TPU v7x, 32 devices: a whole 2x2x4 slice. The times are simulated.
32 devices in a mesh: tm: 8 (over y, x, core), pts: 4 (over z).
Axes of the slice: x: 2, y: 2, z: 4, core: 2. Of those that a mesh axis runs over, the one named last changes fastest.
Arguments:
- snapshots: bfloat16 [16, 512, 5, 1024], P(None, 'tm', None, 'pts'), may hold values from -8 to 8
- weights: float32 [5, 1024], P(None, 'pts'), may hold values from 7.8125e-05 to 0.00078125
- freq_bins: int32 [64], replicated, may hold values from 0 to 255, as said below
- bin_owners: int32 [64], replicated, may hold values from 0 to 7, as said below
Outputs:
- csd: float32 [128, 512], P('tm')
Inputs may be any that keep to these rules, and one draw needn't show every extreme that they name: `freq_bins`: the listed bins are distinct. `bin_owners`: no owner holds more than 16 listed bins and one holds exactly 16; owners hold uneven numbers of bins.
All inputs are finite; a program needn't handle non-finite values.
Results may differ from a plain program's by a relative error of at most 0.00053.
Values may be sent and summed in bfloat16 or wider, within the bound.
A program may use at most 64 MiB of HBM per device.

v0:
```python
import jax
import jax.numpy as jnp
from jax import lax
from jax.sharding import PartitionSpec as P

CAP = 16


def slot_index(bin_owners, owner_count):
    owner_ids = jnp.arange(owner_count, dtype=jnp.int32)
    onehot = (bin_owners[:, None] == owner_ids[None, :]).astype(jnp.int32)
    before = jnp.cumsum(onehot, axis=0) - onehot
    position = jnp.sum(before * onehot, axis=1)
    return bin_owners * CAP + position


def dft_rows(bin_values, live_mask, fft_len):
    steps_t = jnp.arange(fft_len, dtype=jnp.int32)
    wound = bin_values[:, None] * steps_t[None, :] % fft_len
    angles = 2.0 * jnp.pi * wound.astype(jnp.float32) / fft_len
    hann_window = 0.5 - 0.5 * jnp.cos(2.0 * jnp.pi * steps_t.astype(jnp.float32) / fft_len)
    scaled = hann_window / jnp.sqrt(jnp.float32(3.0 * fft_len / 8.0))
    scaled = scaled[None, :] * live_mask[:, None]
    cosine = (scaled * jnp.cos(angles)).astype(jnp.bfloat16)
    sine_rows = (-scaled * jnp.sin(angles)).astype(jnp.bfloat16)
    return jnp.stack([cosine, sine_rows], axis=1).reshape(-1, fft_len)


def fold_gram(gram_mat, blocks):
    real_part = gram_mat[..., :blocks, :blocks] + gram_mat[..., blocks:, blocks:]
    imag_part = gram_mat[..., :blocks, blocks:] - gram_mat[..., blocks:, :blocks]
    leading = gram_mat.shape[:-2]
    return jnp.concatenate(
        [
            real_part.reshape(leading + (blocks * blocks,)),
            imag_part.reshape(leading + (blocks * blocks,)),
        ],
        axis=-1,
    )


def shards(snapshots, weights, freq_bins, bin_owners):
    blocks, local_steps, fields, points = snapshots.shape
    tm_count = lax.axis_size("tm")
    fft_len = local_steps * tm_count
    sub_points = points // tm_count
    slot_count = tm_count * CAP
    by_point = lax.all_to_all(snapshots, "tm", split_axis=3, concat_axis=1, tiled=True)
    by_point = by_point.reshape(blocks, fft_len, fields * sub_points)
    slot_ids = slot_index(bin_owners, tm_count)
    matches = slot_ids[None, :] == jnp.arange(slot_count, dtype=jnp.int32)[:, None]
    is_live = jnp.any(matches, axis=1).astype(jnp.float32)
    slot_bins = jnp.sum(jnp.where(matches, freq_bins[None, :], 0), axis=1)
    dft_table = dft_rows(slot_bins, is_live, fft_len)
    spectra = jnp.einsum(
        "st,btc->sbc", dft_table, by_point, preferred_element_type=jnp.float32
    ).astype(jnp.bfloat16)
    spectra = spectra.reshape(tm_count, CAP, 2 * blocks, fields * sub_points)
    owner_weights = jnp.transpose(weights.reshape(fields, tm_count, sub_points), (1, 0, 2)).reshape(
        -1
    )
    spectra_part = lax.all_to_all(spectra, "tm", split_axis=0, concat_axis=3, tiled=True)[0]
    weighted = (spectra_part * owner_weights).astype(jnp.bfloat16)
    gram_mat = jnp.einsum(
        "kac,kbc->kab", spectra_part, weighted, preferred_element_type=jnp.float32
    )
    partial_value = fold_gram(gram_mat, blocks)
    summed = lax.psum(partial_value, "pts")
    return summed


def solution(mesh):
    in_specs = (P(None, "tm", None, "pts"), P(None, "pts"), P(), P())
    out_specs = P("tm", None)
    return jax.shard_map(shards, mesh=mesh, in_specs=in_specs, out_specs=out_specs, check_vma=False)
```

profile of v0, /device:TPU:0, one launch (start us, length us, event | category | flops | bytes accessed | tf_op | source)
XLA Modules:
  0.0 135.6 jit_solution(8680687108068452311)
XLA Ops:
  0.0 7.6 %copy.36 = bf16[16,64,5,256]{1,0,2,3:T(8,128)(2,1)} copy(bf16[16,64,5,256]{3,1,2,0:T(8,128)(2,1)} %param.4) | data formatting | bytes 5242880 | tf_op args[0]
  7.6 8.2 %reshape.225 = bf16[8,2,81920]{2,1,0:T(2,128)(2,1)} reshape(bf16[256,5,16,64]{3,2,1,0:T(8,128)(2,1)} %bitcast.26) | data formatting | bytes 5242880
  15.9 5.3 %all-to-all-start = ((bf16[8,2,81920]{2,1,0:T(2,128)(2,1)}), bf16[8,2,81920]{2,1,0:T(2,128)(2,1)S(1)}, u32[]{:S(2)}, u32[]{:S(2)}) async-start(bf16[8,2,81920]{2,1,0:T(2,128)(2,1)} %reshape.225), calls=%async_computation | async-start | bytes 5242880 | tf_op jit(solution)/shard_map/all_to_all | solution.py:48
  21.2 0.0 copy-done.1
  21.2 0.1 fusion.12
  21.2 0.1 reduce_window_sum.11
  21.3 0.2 select_reduce_fusion.1
  21.5 0.1 fusion.11
  21.7 0.0 copy-done.2
  21.7 0.1 select_reduce_fusion
  21.8 1.3 fusion.2
  23.1 0.3 copy.35
  23.4 0.1 reshape.217
  23.5 29.9 %all-to-all-done = bf16[8,2,81920]{2,1,0:T(2,128)(2,1)S(1)} async-done(((bf16[8,2,81920]{2,1,0:T(2,128)(2,1)}), bf16[8,2,81920]{2,1,0:T(2,128)(2,1)S(1)}, u32[]{:S(2)}, u32[]{:S(2)}) %all-to-all-start) | async-done | bytes 2621472 | tf_op jit(solution)/shard_map/all_to_all | solution.py:48
  53.4 5.5 %reshape.226 = bf16[256,5,16,64]{3,2,1,0:T(8,128)(2,1)} reshape(bf16[8,2,81920]{2,1,0:T(2,128)(2,1)S(1)} %all-to-all-done) | data formatting | bytes 5242880
  59.0 8.2 %copy.38 = bf16[16,8,64,5,32]{2,1,4,3,0:T(8,128)(2,1)} copy(bf16[16,8,64,5,32]{2,0,3,4,1:T(8,128)(2,1)} %bitcast.25) | data formatting | bytes 5242880 | tf_op jit(solution)/shard_map/all_to_all | solution.py:48
  67.2 6.7 %reshape.218 = bf16[16,512,160]{1,2,0:T(8,128)(2,1)S(1)} reshape(bf16[16,8,64,5,32]{2,1,4,3,0:T(8,128)(2,1)} %copy.38) | data formatting | bytes 5242880 | tf_op jit(solution)/shard_map/reshape | solution.py:49
  73.9 0.9 fusion.13
  74.7 0.2 convert_element_type.66
  74.9 3.1 %copy.39 = bf16[256,16,160]{2,1,0:T(8,128)(2,1)} copy(bf16[256,16,160]{0,2,1:T(8,128)(2,1)S(1)} %convert_element_type.66) | data formatting | bytes 2621440 | tf_op jit(solution)/shard_map/convert_element_type | solution.py:57
  78.0 3.9 %all-to-all-start.1 = ((bf16[8,16,32,160]{3,2,1,0:T(8,128)(2,1)}), bf16[8,16,32,160]{3,2,1,0:T(8,128)(2,1)S(1)}, u32[]{:S(2)}, u32[]{:S(2)}) async-start(bf16[8,16,32,160]{3,2,1,0:T(8,128)(2,1)} %bitcast.30), calls=%async_computation.1 | async-start | bytes 4194304 | tf_op jit(solution)/shard_map/all_to_all | solution.py:62
  81.9 0.0 copy-done
  81.9 0.1 reshape.220
  82.0 0.1 mul.111
  82.1 26.2 %all-to-all-done.1 = bf16[8,16,32,160]{3,2,1,0:T(8,128)(2,1)S(1)} async-done(((bf16[8,16,32,160]{3,2,1,0:T(8,128)(2,1)}), bf16[8,16,32,160]{3,2,1,0:T(8,128)(2,1)S(1)}, u32[]{:S(2)}, u32[]{:S(2)}) %all-to-all-start.1) | async-done | bytes 1310752 | tf_op jit(solution)/shard_map/all_to_all | solution.py:62
  108.3 2.8 %copy.40 = bf16[1,16,32,8,160]{4,3,2,1,0:T(8,128)(2,1)} copy(bf16[1,16,32,8,160]{4,2,1,3,0:T(8,128)(2,1)S(1)} %bitcast.29) | data formatting | bytes 2621440 | tf_op jit(solution)/shard_map/all_to_all | solution.py:62
  111.1 3.8 %squeeze.3 = bf16[16,32,1280]{2,1,0:T(8,128)(2,1)S(1)} reshape(bf16[1,16,32,8,160]{4,3,2,1,0:T(8,128)(2,1)} %copy.40) | data formatting | bytes 2621440 | tf_op jit(solution)/shard_map/squeeze | solution.py:62
  114.8 0.5 fusion
  115.3 0.1 slice_add_fusion
  115.5 0.1 reshape.221
  115.6 0.1 reshape.222
  115.7 19.8 %psum.7 = f32[16,512]{1,0:T(8,128)} all-reduce(f32[16,512]{1,0:T(8,128)S(1)} %pad_maximum_fusion.1), channel_id=1, replica_groups=mesh['tm'=8,'pts'=4] {'pts'}, use_global_device_ids=true, to_apply=%region_4.5 | all-reduce | flops 8192 | bytes 65536 | tf_op jit(solution)/shard_map/psum | solution.py:68
  (9 shorter events, 0.1 us)
Async XLA Ops:
  15.9 5.3 %copy-start.1 = (s32[64]{0:T(128)S(1)}, s32[64]{0:T(128)}, u32[]{:S(2)}) copy-start(s32[64]{0:T(128)} %param.7) | copy-start | bytes 772
  15.9 5.8 %copy-start.2 = (s32[64]{0:T(128)S(1)}, s32[64]{0:T(128)}, u32[]{:S(2)}) copy-start(s32[64]{0:T(128)} %param.6) | copy-start | bytes 772
  15.9 37.6 %all-to-all-start = ((bf16[8,2,81920]{2,1,0:T(2,128)(2,1)}), bf16[8,2,81920]{2,1,0:T(2,128)(2,1)S(1)}, u32[]{:S(2)}, u32[]{:S(2)}) async-start(bf16[8,2,81920]{2,1,0:T(2,128)(2,1)} %reshape.225), calls=%async_computation | async-start | bytes 5242880 | tf_op jit(solution)/shard_map/all_to_all | solution.py:48
  78.0 3.9 %copy-start = (f32[5,256]{1,0:T(8,128)S(1)}, f32[5,256]{1,0:T(8,128)}, u32[]{:S(2)}) copy-start(f32[5,256]{1,0:T(8,128)} %param.5) | copy-start | bytes 15364
  78.0 30.3 %all-to-all-start.1 = ((bf16[8,16,32,160]{3,2,1,0:T(8,128)(2,1)}), bf16[8,16,32,160]{3,2,1,0:T(8,128)(2,1)S(1)}, u32[]{:S(2)}, u32[]{:S(2)}) async-start(bf16[8,16,32,160]{3,2,1,0:T(8,128)(2,1)} %bitcast.30), calls=%async_computation.1 | async-start | bytes 4194304 | tf_op jit(solution)/shard_map/all_to_all | solution.py:62
where the time goes:
time: 136 us
  waiting for transfers between devices  56.1 us (41%)
  local copies, waits for them, and re-layouts  46.7 us (34%)
  blocking collectives  19.8 us (15%)
  starting transfers between devices  9.22 us (7%)
  other arithmetic  2.23 us (2%)
    all_to_all x1, waiting for transfers between devices, shards(): lax.all_to_all(snapshots, 'tm', split_axis=3, concat_axis=1, tiled=True)  29.9 us
    all_to_all x1, waiting for transfers between devices, shards(): lax.all_to_all(spectra, 'tm', split_axis=0, concat_axis=3, tiled=True)[0]  26.2 us
    unnamed x9, local copies, waits for them, and re-layouts  21.4 us
    psum x1, blocking collectives, shards(): summed = lax.psum(partial_value, 'pts')  19.8 us
    all_to_all x1, local copies, waits for them, and re-layouts, shards(): lax.all_to_all(snapshots, 'tm', split_axis=3, concat_axis=1, tiled=True)  8.21 us
    reshape x1, local copies, waits for them, and re-layouts, shards(): by_point = by_point.reshape(blocks, fft_len, fields * sub_points)  6.71 us
    all_to_all x1, starting transfers between devices, shards(): lax.all_to_all(snapshots, 'tm', split_axis=3, concat_axis=1, tiled=True)  5.3 us
    all_to_all x1, starting transfers between devices, shards(): lax.all_to_all(spectra, 'tm', split_axis=0, concat_axis=3, tiled=True)[0]  3.91 us
  transfers between devices with their start and end apart: 2, of which 2 were waited for; matrix products, arithmetic and copies ran while one was open for 2% of the time, Pallas kernels for 0%

commit v1 on v0

--- a/solution.py
+++ b/solution.py
@@ -48,25 +48,22 @@
     by_point = lax.all_to_all(snapshots, "tm", split_axis=3, concat_axis=1, tiled=True)
     by_point = by_point.reshape(blocks, fft_len, fields * sub_points)
     slot_ids = slot_index(bin_owners, tm_count)
-    matches = slot_ids[None, :] == jnp.arange(slot_count, dtype=jnp.int32)[:, None]
-    is_live = jnp.any(matches, axis=1).astype(jnp.float32)
-    slot_bins = jnp.sum(jnp.where(matches, freq_bins[None, :], 0), axis=1)
-    dft_table = dft_rows(slot_bins, is_live, fft_len)
+    ones = jnp.ones(freq_bins.shape, jnp.float32)
+    dft_table = dft_rows(freq_bins, ones, fft_len)
     spectra = jnp.einsum(
         "st,btc->sbc", dft_table, by_point, preferred_element_type=jnp.float32
     ).astype(jnp.bfloat16)
-    spectra = spectra.reshape(tm_count, CAP, 2 * blocks, fields * sub_points)
-    owner_weights = jnp.transpose(weights.reshape(fields, tm_count, sub_points), (1, 0, 2)).reshape(
-        -1
-    )
-    spectra_part = lax.all_to_all(spectra, "tm", split_axis=0, concat_axis=3, tiled=True)[0]
-    weighted = (spectra_part * owner_weights).astype(jnp.bfloat16)
-    gram_mat = jnp.einsum(
-        "kac,kbc->kab", spectra_part, weighted, preferred_element_type=jnp.float32
-    )
+    spectra = spectra.reshape(freq_bins.shape[0], 2, blocks, fields * sub_points)
+    me = lax.axis_index("tm")
+    own = lax.dynamic_slice_in_dim(weights, me * sub_points, sub_points, axis=1).reshape(-1)
+    spectra = spectra.reshape(freq_bins.shape[0], 2 * blocks, fields * sub_points)
+    weighted = (spectra * own).astype(jnp.bfloat16)
+    gram_mat = jnp.einsum("kac,kbc->kab", spectra, weighted, preferred_element_type=jnp.float32)
     partial_value = fold_gram(gram_mat, blocks)
-    summed = lax.psum(partial_value, "pts")
-    return summed
+    summed = lax.psum(partial_value, ("tm", "pts"))
+    own_slots = me * CAP + jnp.arange(CAP, dtype=jnp.int32)
+    matches = (own_slots[:, None] == slot_ids[None, :]).astype(jnp.float32)
+    return jnp.dot(matches, summed, precision=lax.Precision.HIGHEST)
 
 
 def solution(mesh):

time: 136 us -> 218 us (1.60)
  waiting for transfers between devices: 56.1 us -> 155 us
  blocking collectives: 19.8 us -> 0 us
  between operations: 0.14 us -> 13.5 us
  local copies, waits for them, and re-layouts: 46.7 us -> 38.2 us
  starting transfers between devices: 9.22 us -> 5.34 us
    psum x0 -> x1, waiting for transfers between devices: none -> 125 us  [shards(): summed = lax.psum(partial_value, ('tm', 'pts'))]
    all_to_all x1 -> x0, waiting for transfers between devices: 26.2 us -> none  [shards(): lax.all_to_all(spectra, 'tm', split_axis=0, concat_axis=3, tiled=True)[0]]
    psum x1 -> x0, blocking collectives: 19.8 us -> none  [shards(): summed = lax.psum(partial_value, 'pts')]
    all_to_all x1 -> x0, starting transfers between devices: 3.91 us -> none  [shards(): lax.all_to_all(spectra, 'tm', split_axis=0, concat_axis=3, tiled=True)[0]]
    squeeze x1 -> x0, local copies, waits for them, and re-layouts: 3.78 us -> none  [shards(): lax.all_to_all(spectra, 'tm', split_axis=0, concat_axis=3, tiled=True)[0]]
    all_to_all x1 -> x0, local copies, waits for them, and re-layouts: 2.77 us -> none  [shards(): lax.all_to_all(spectra, 'tm', split_axis=0, concat_axis=3, tiled=True)[0]]
  transfers between devices with their start and end apart: 2 -> 2, of which waited for: 2 -> 2; matrix products, arithmetic and copies ran while one was open for 2% -> 1% of each run, Pallas kernels for 0% -> 0%
where the time goes in v1:
time: 218 us
  waiting for transfers between devices  155 us (71%)
  local copies, waits for them, and re-layouts  38.2 us (18%)
  between operations  13.5 us (6%)
  starting transfers between devices  5.34 us (2%)
  matrix products  3.08 us (1%)
  other arithmetic  2.18 us (1%)
    psum x1, waiting for transfers between devices, shards(): summed = lax.psum(partial_value, ('tm', 'pts'))  125 us
    all_to_all x1, waiting for transfers between devices, shards(): lax.all_to_all(snapshots, 'tm', split_axis=3, concat_axis=1, tiled=True)  30.8 us
    unnamed x9, local copies, waits for them, and re-layouts  21.5 us
    all_to_all x1, local copies, waits for them, and re-layouts, shards(): lax.all_to_all(snapshots, 'tm', split_axis=3, concat_axis=1, tiled=True)  8.19 us
    reshape x1, local copies, waits for them, and re-layouts, shards(): by_point = by_point.reshape(blocks, fft_len, fields * sub_points)  6.71 us
    all_to_all x1, starting transfers between devices, shards(): lax.all_to_all(snapshots, 'tm', split_axis=3, concat_axis=1, tiled=True)  5.3 us
  transfers between devices with their start and end apart: 2, of which 2 were waited for; matrix products, arithmetic and copies ran while one was open for 1% of the time, Pallas kernels for 0%

profile of v1, /device:TPU:0, one launch (start us, length us, event | category | flops | bytes accessed | tf_op | source)
XLA Modules:
  0.0 217.6 jit_solution(3894541752250214509)
XLA Ops:
  6.5 0.0 copy-start
  6.5 7.8 %copy.30 = bf16[16,64,5,256]{1,0,2,3:T(8,128)(2,1)} copy(bf16[16,64,5,256]{3,1,2,0:T(8,128)(2,1)} %param.4) | data formatting | bytes 5242880 | tf_op args[0]
  14.3 8.2 %reshape.172 = bf16[8,2,81920]{2,1,0:T(2,128)(2,1)} reshape(bf16[256,5,16,64]{3,2,1,0:T(8,128)(2,1)} %bitcast.21) | data formatting | bytes 5242880
  22.5 0.0 copy-start.2
  22.5 5.3 %all-to-all-start = ((bf16[8,2,81920]{2,1,0:T(2,128)(2,1)}), bf16[8,2,81920]{2,1,0:T(2,128)(2,1)S(1)}, u32[]{:S(2)}, u32[]{:S(2)}) async-start(bf16[8,2,81920]{2,1,0:T(2,128)(2,1)} %reshape.172), calls=%async_computation | async-start | bytes 5242880 | tf_op jit(solution)/shard_map/all_to_all | solution.py:48
  27.8 0.0 all-reduce.2.cloned.1.call-start
  27.9 0.0 copy-done.2
  27.9 0.6 multiply_convert_fusion.3
  28.6 0.1 copy.29
  28.7 0.1 reshape.166
  28.8 0.0 copy-done
  28.8 0.1 constant_dynamic-slice_fusion
  28.8 0.1 mul.103
  28.9 0.0 copy-done.1
  28.9 0.1 fusion.8
  29.0 0.1 reduce_window_sum.11
  29.1 0.2 select_reduce_fusion
  29.3 30.8 %all-to-all-done = bf16[8,2,81920]{2,1,0:T(2,128)(2,1)S(1)} async-done(((bf16[8,2,81920]{2,1,0:T(2,128)(2,1)}), bf16[8,2,81920]{2,1,0:T(2,128)(2,1)S(1)}, u32[]{:S(2)}, u32[]{:S(2)}) %all-to-all-start) | async-done | bytes 2621472 | tf_op jit(solution)/shard_map/all_to_all | solution.py:48
  60.1 5.6 %reshape.173 = bf16[256,5,16,64]{3,2,1,0:T(8,128)(2,1)} reshape(bf16[8,2,81920]{2,1,0:T(2,128)(2,1)S(1)} %all-to-all-done) | data formatting | bytes 5242880
  65.6 8.2 %copy.32 = bf16[16,8,64,5,32]{2,1,4,3,0:T(8,128)(2,1)} copy(bf16[16,8,64,5,32]{2,0,3,4,1:T(8,128)(2,1)} %bitcast.20) | data formatting | bytes 5242880 | tf_op jit(solution)/shard_map/all_to_all | solution.py:48
  73.8 6.7 %reshape.167 = bf16[16,512,160]{1,2,0:T(8,128)(2,1)S(1)} reshape(bf16[16,8,64,5,32]{2,1,4,3,0:T(8,128)(2,1)} %copy.32) | data formatting | bytes 5242880 | tf_op jit(solution)/shard_map/reshape | solution.py:49
  80.6 0.8 fusion.14
  81.4 0.1 convert_element_type.61
  81.5 0.9 copy.33
  82.4 0.4 fusion
  82.8 0.3 slice_add_fusion
  83.1 0.2 copy.35
  83.4 0.2 copy.34
  83.6 0.7 pad_maximum_fusion
  84.4 0.0 all-reduce.2.cloned.1.call-update
  84.4 124.5 %all-reduce.2.cloned.1.call-done = f32[64,512]{0,1:T(8,128)} async-done(((f32[64,512]{0,1:T(8,128)}), f32[64,512]{0,1:T(8,128)}) %all-reduce.2.cloned.1.call-update) | async-done | bytes 131088 | tf_op jit(solution)/shard_map/psum | solution.py:63
  208.9 1.8 fusion.9
  (5 shorter events, 0.1 us)
Async XLA Ops:
  6.5 22.2 %copy-start = (f32[5,256]{1,0:T(8,128)S(1)}, f32[5,256]{1,0:T(8,128)}, u32[]{:S(2)}) copy-start(f32[5,256]{1,0:T(8,128)} %param.5) | copy-start | bytes 15364
  22.5 5.4 %copy-start.2 = (s32[64]{0:T(128)S(1)}, s32[64]{0:T(128)}, u32[]{:S(2)}) copy-start(s32[64]{0:T(128)} %param.6) | copy-start | bytes 772
  22.5 6.4 %copy-start.1 = (s32[64]{0:T(128)S(1)}, s32[64]{0:T(128)}, u32[]{:S(2)}) copy-start(s32[64]{0:T(128)} %param.7) | copy-start | bytes 772
  22.5 37.6 %all-to-all-start = ((bf16[8,2,81920]{2,1,0:T(2,128)(2,1)}), bf16[8,2,81920]{2,1,0:T(2,128)(2,1)S(1)}, u32[]{:S(2)}, u32[]{:S(2)}) async-start(bf16[8,2,81920]{2,1,0:T(2,128)(2,1)} %reshape.172), calls=%async_computation | async-start | bytes 5242880 | tf_op jit(solution)/shard_map/all_to_all | solution.py:48
  27.8 181.1 %all-reduce.2.cloned.1.call-start = ((), (), s32[]{:S(2)}) async-start(), calls=%async_computation.1 | async-start | bytes 524288 | tf_op jit(solution)/shard_map/psum | solution.py:63
Sparse Core Ops, SparseCore 0:
  84.5 124.3 all-reduce.1

commit v2 on v1

v2 whole, which is shorter than its diff:
```python
import functools

import jax
import jax.numpy as jnp
from jax import lax
from jax.experimental import pallas as pl
from jax.experimental.pallas import tpu as pltpu
from jax.sharding import PartitionSpec as P

CAP = 16
MESH = pl.DeviceIdType.MESH
LANES = 128
VMEM_BYTES = 40 * 1024 * 1024


def slot_index(bin_owners, owner_count):
    owner_ids = jnp.arange(owner_count, dtype=jnp.int32)
    onehot = (bin_owners[:, None] == owner_ids[None, :]).astype(jnp.int32)
    before = jnp.cumsum(onehot, axis=0) - onehot
    position = jnp.sum(before * onehot, axis=1)
    return bin_owners * CAP + position


def dft_rows(bin_values, fft_len):
    steps_t = jnp.arange(fft_len, dtype=jnp.int32)
    wound = bin_values[:, None] * steps_t[None, :] % fft_len
    angles = 2.0 * jnp.pi * wound.astype(jnp.float32) / fft_len
    hann_window = 0.5 - 0.5 * jnp.cos(2.0 * jnp.pi * steps_t.astype(jnp.float32) / fft_len)
    scaled = hann_window / jnp.sqrt(jnp.float32(3.0 * fft_len / 8.0))
    scaled = scaled[None, :]
    cosine = (scaled * jnp.cos(angles)).astype(jnp.bfloat16)
    sine_rows = (-scaled * jnp.sin(angles)).astype(jnp.bfloat16)
    return jnp.concatenate([cosine, sine_rows], axis=0)


def fold_gram(gram_mat, blocks):
    real_part = gram_mat[..., :blocks, :blocks] + gram_mat[..., blocks:, blocks:]
    imag_part = gram_mat[..., :blocks, blocks:] - gram_mat[..., blocks:, :blocks]
    leading = gram_mat.shape[:-2]
    return jnp.concatenate(
        [
            real_part.reshape(leading + (blocks * blocks,)),
            imag_part.reshape(leading + (blocks * blocks,)),
        ],
        axis=-1,
    )


def exchange_kernel(count, x_ref, table_ref, spec_ref, send, held, send_sem, recv_sem):
    blocks, fields, steps, points = x_ref.shape
    sub = points // count
    group = LANES // sub
    me = lax.axis_index("tm")
    barrier = pltpu.get_barrier_semaphore()
    for k in range(1, count):
        pl.semaphore_signal(
            barrier, inc=1, device_id={"tm": lax.rem(me + k, count)}, device_id_type=MESH
        )
    for tile in range(blocks * fields // group):
        rows = [x_ref[j // fields, j % fields] for j in range(tile * group, (tile + 1) * group)]
        for d in range(count):
            packed = jnp.concatenate([r[:, d * sub : (d + 1) * sub] for r in rows], axis=1)
            send[d, :, tile * LANES : (tile + 1) * LANES] = packed
    pl.semaphore_wait(barrier, count - 1)
    copies = []
    for k in range(1, count):
        peer = lax.rem(me + k, count)
        copy = pltpu.make_async_remote_copy(
            src_ref=send.at[peer],
            dst_ref=held.at[me],
            send_sem=send_sem.at[k],
            recv_sem=recv_sem.at[k],
            device_id={"tm": peer},
            device_id_type=MESH,
        )
        copy.start()
        copies.append(copy)
    held[me] = send[me]
    for k in range(1, count):
        source = lax.rem(me + count - k, count)
        pltpu.make_async_remote_copy(
            src_ref=send.at[source],
            dst_ref=held.at[source],
            send_sem=send_sem.at[k],
            recv_sem=recv_sem.at[k],
            device_id={"tm": source},
            device_id_type=MESH,
        ).wait_recv()
    columns = held.shape[2]
    width = LANES * (5 if (columns // LANES) % 5 == 0 else 1)
    for c in range(columns // width):
        part = held[:, :, c * width : (c + 1) * width].reshape(count * steps, width)
        out = jnp.dot(table_ref[...], part, preferred_element_type=jnp.float32)
        spec_ref[:, c * width : (c + 1) * width] = out.astype(jnp.bfloat16)
    for copy in copies:
        copy.wait_send()


def exchange(by_field, table, count):
    blocks, fields, steps, points = by_field.shape
    columns = blocks * fields * points // count
    return pl.pallas_call(
        functools.partial(exchange_kernel, count),
        out_shape=jax.ShapeDtypeStruct((table.shape[0], columns), jnp.bfloat16),
        in_specs=[pl.BlockSpec(memory_space=pltpu.VMEM)] * 2,
        out_specs=pl.BlockSpec(memory_space=pltpu.VMEM),
        scratch_shapes=[
            pltpu.VMEM((count, steps, columns), jnp.bfloat16),
            pltpu.VMEM((count, steps, columns), jnp.bfloat16),
            pltpu.SemaphoreType.DMA((count,)),
            pltpu.SemaphoreType.DMA((count,)),
        ],
        compiler_params=pltpu.CompilerParams(
            collective_id=0, has_side_effects=True, vmem_limit_bytes=VMEM_BYTES
        ),
    )(by_field, table)


def reduce_kernel(count, depth, part_ref, out_ref, first, second, s1, r1, s2, r2):
    me, here = lax.axis_index("tm"), lax.axis_index("pts")
    barrier = pltpu.get_barrier_semaphore()
    for k in range(1, count):
        pl.semaphore_signal(
            barrier, inc=1, device_id={"tm": lax.rem(me + k, count)}, device_id_type=MESH
        )
    for k in range(1, depth):
        pl.semaphore_signal(
            barrier, inc=1, device_id={"pts": lax.rem(here + k, depth)}, device_id_type=MESH
        )
    pl.semaphore_wait(barrier, count + depth - 2)

    def over(axis, position, size, source, dest, send_sem, recv_sem):
        copies = []
        for k in range(1, size):
            peer = lax.rem(position + k, size)
            copy = pltpu.make_async_remote_copy(
                src_ref=source(peer),
                dst_ref=dest.at[position],
                send_sem=send_sem.at[k],
                recv_sem=recv_sem.at[k],
                device_id={axis: peer},
                device_id_type=MESH,
            )
            copy.start()
            copies.append(copy)
        dest[position] = source(position)[...]
        for k in range(1, size):
            origin = lax.rem(position + size - k, size)
            pltpu.make_async_remote_copy(
                src_ref=source(origin),
                dst_ref=dest.at[origin],
                send_sem=send_sem.at[k],
                recv_sem=recv_sem.at[k],
                device_id={axis: origin},
                device_id_type=MESH,
            ).wait_recv()
        total = dest[0]
        for k in range(1, size):
            total = total + dest[k]
        for copy in copies:
            copy.wait_send()
        return total

    total = over("tm", me, count, lambda d: part_ref.at[d], first, s1, r1)
    out_ref[...] = total
    out_ref[...] = over("pts", here, depth, lambda d: out_ref, second, s2, r2)


def reduce_slots(part, count, depth):
    cap, width = part.shape[1:]
    return pl.pallas_call(
        functools.partial(reduce_kernel, count, depth),
        out_shape=jax.ShapeDtypeStruct((cap, width), jnp.float32),
        in_specs=[pl.BlockSpec(memory_space=pltpu.VMEM)],
        out_specs=pl.BlockSpec(memory_space=pltpu.VMEM),
        scratch_shapes=[
            pltpu.VMEM((count, cap, width), jnp.float32),
            pltpu.VMEM((depth, cap, width), jnp.float32),
            pltpu.SemaphoreType.DMA((count,)),
            pltpu.SemaphoreType.DMA((count,)),
            pltpu.SemaphoreType.DMA((depth,)),
            pltpu.SemaphoreType.DMA((depth,)),
        ],
        compiler_params=pltpu.CompilerParams(
            collective_id=1, has_side_effects=True, vmem_limit_bytes=VMEM_BYTES
        ),
    )(part)


def shards(snapshots, weights, freq_bins, bin_owners):
    blocks, local_steps, fields, points = snapshots.shape
    tm_count = lax.axis_size("tm")
    pts_count = lax.axis_size("pts")
    listed = freq_bins.shape[0]
    sub_points = points // tm_count
    slot_count = tm_count * CAP
    table = dft_rows(freq_bins, local_steps * tm_count)
    spectra = exchange(jnp.transpose(snapshots, (0, 2, 1, 3)), table, tm_count)
    spectra = spectra.reshape(2, listed, blocks, fields * sub_points)
    me = lax.axis_index("tm")
    own = lax.dynamic_slice_in_dim(weights, me * sub_points, sub_points, axis=1).reshape(-1)
    spectra = jnp.transpose(spectra, (1, 0, 2, 3)).reshape(listed, 2 * blocks, -1)
    weighted = (spectra * own).astype(jnp.bfloat16)
    gram_mat = jnp.einsum("kac,kbc->kab", spectra, weighted, preferred_element_type=jnp.float32)
    partial_value = fold_gram(gram_mat, blocks)
    slot_ids = slot_index(bin_owners, tm_count)
    matches = slot_ids[None, :] == jnp.arange(slot_count, dtype=jnp.int32)[:, None]
    placed = jnp.dot(
        matches.astype(jnp.float32), partial_value, precision=lax.Precision.HIGHEST
    )
    return reduce_slots(placed.reshape(tm_count, CAP, -1), tm_count, pts_count)


def solution(mesh):
    in_specs = (P(None, "tm", None, "pts"), P(None, "pts"), P(), P())
    out_specs = P("tm", None)
    return jax.shard_map(shards, mesh=mesh, in_specs=in_specs, out_specs=out_specs, check_vma=False)
```

time: 218 us -> 54.2 us (0.25)
  waiting for transfers between devices: 155 us -> 0 us
  Pallas kernels: 0 us -> 46.7 us
  local copies, waits for them, and re-layouts: 38.2 us -> 4.44 us
  between operations: 13.5 us -> 0.11 us
  starting transfers between devices: 5.34 us -> 0 us
  matrix products: 3.08 us -> 0.74 us
    psum x1 -> x0, waiting for transfers between devices: 125 us -> none  [shards(): summed = lax.psum(partial_value, ('tm', 'pts'))]
    pallas_call x0 -> x2, Pallas kernels: none -> 46.7 us  [the longest x1 32.7 us: exchange(): pl.pallas_call(functools.partial(exchange_kernel, count), out_shape=jax.S...]
    all_to_all x1 -> x0, waiting for transfers between devices: 30.8 us -> none  [shards(): lax.all_to_all(snapshots, 'tm', split_axis=3, concat_axis=1, tiled=True)]
    unnamed x9 -> x7, local copies, waits for them, and re-layouts: 21.5 us -> 2.36 us
    all_to_all x1 -> x0, local copies, waits for them, and re-layouts: 8.19 us -> none  [shards(): lax.all_to_all(snapshots, 'tm', split_axis=3, concat_axis=1, tiled=True)]
    reshape x2 -> x1, local copies, waits for them, and re-layouts: 6.76 us -> 1.3 us  [shards(): spectra = spectra.reshape(2, listed, blocks, fields * sub_points)]
    all_to_all x1 -> x0, starting transfers between devices: 5.3 us -> none  [shards(): lax.all_to_all(snapshots, 'tm', split_axis=3, concat_axis=1, tiled=True)]
  transfers between devices with their start and end apart: 2 -> 0, of which waited for: 2 -> 0; matrix products, arithmetic and copies ran while one was open for 1% -> 0% of each run, Pallas kernels for 0% -> 0%
where the time goes in v2:
time: 54.2 us; the launch traced here: 54 us
  Pallas kernels  46.7 us (86%)
  local copies, waits for them, and re-layouts  4.44 us (8%)
  other arithmetic  2 us (4%)
  matrix products  0.74 us (1%)
    pallas_call x1, Pallas kernels, exchange(): pl.pallas_call(functools.partial(exchange_kernel, count), out_shape=jax.S...  32.7 us
    pallas_call x1, Pallas kernels, reduce_slots(): pl.pallas_call(functools.partial(reduce_kernel, count, depth), out_shape=...  14 us
    unnamed x7, local copies, waits for them, and re-layouts  2.36 us
    reshape x1, local copies, waits for them, and re-layouts, shards(): spectra = spectra.reshape(2, listed, blocks, fields * sub_points)  1.3 us
    convert_element_type x1, other arithmetic, dft_rows(): cosine = (scaled * jnp.cos(angles)).astype(jnp.bfloat16)  1.26 us

profile of v2, /device:TPU:0, one launch (start us, length us, event | category | flops | bytes accessed | tf_op | source)
XLA Modules:
  0.0 54.0 jit_solution(11823569719327415955)
XLA Ops:
  0.0 0.0 copy-start
  0.0 1.3 %multiply_convert_fusion.3 = (bf16[64,512]{1,0:T(8,128)(2,1)S(1)}, bf16[64,512]{1,0:T(8,128)(2,1)S(1)}) fusion(s32[64]{0:T(128)} %param.6, f32[512]{0:T(512)S(1)} %get-tuple-element.9, f32[512]{0:T(512)S(1)} %get-tuple-element.10), kind=kLoop, calls=%fused_computation.17 | loop fusion | flops 589824 | bytes 135424 | tf_op jit(solution)/shard_map/convert_element_type | solution.py:31
  1.3 0.0 copy-start.1
  1.3 1.7 %copy-done.1 = bf16[16,64,5,256]{3,1,2,0:T(8,128)(2,1)S(1)} copy-done((bf16[16,64,5,256]{3,1,2,0:T(8,128)(2,1)S(1)}, bf16[16,64,5,256]{3,1,2,0:T(8,128)(2,1)}, u32[]{:S(2)}) %copy-start.1) | copy-done | bytes 2621464
  3.1 32.7 %shard_map.46 = bf16[128,2560]{1,0:T(8,128)(2,1)S(1)} custom-call(bf16[16,5,64,256]{3,2,1,0:T(8,128)(2,1)S(1)} %bitcast.7, bf16[128,512]{1,0:T(8,128)(2,1)S(1)} %pad_maximum_fusion.table_ref), custom_call_target="tpu_custom_call" | custom-call | tf_op jit(solution)/shard_map/pallas_call | solution.py:102
  35.8 1.3 %reshape.32 = bf16[2,64,16,160]{3,2,1,0:T(8,128)(2,1)S(1)} reshape(bf16[128,2560]{1,0:T(8,128)(2,1)S(1)} %shard_map.46) | data formatting | bytes 1310720 | tf_op jit(solution)/shard_map/reshape | solution.py:199
  37.1 0.1 copy.6
  37.2 0.0 copy-done
  37.2 0.1 constant_dynamic-slice_fusion
  37.3 0.1 mul.81
  37.4 0.4 fusion
  37.8 0.0 copy-start.2
  37.8 0.3 slice_add_fusion
  38.2 0.2 copy.7
  38.4 0.2 copy.8
  38.7 0.0 copy-done.2
  38.7 0.1 fusion.13
  38.7 0.1 reduce_window_sum.11
  38.8 0.2 select_reduce_fusion
  39.0 0.3 fusion.2
  39.3 14.0 %shard_map.47 = f32[16,512]{1,0:T(8,128)S(1)} custom-call(f32[8,16,512]{2,1,0:T(8,128)S(1)} %bitcast.8), custom_call_target="tpu_custom_call" | custom-call | tf_op jit(solution)/shard_map/pallas_call | solution.py:171
  53.4 0.6 %copy.10 = f32[16,512]{1,0:T(8,128)} copy(f32[16,512]{1,0:T(8,128)S(1)} %shard_map.47) | data formatting | bytes 65536
  (3 shorter events, 0.1 us)
Async XLA Ops:
  0.0 37.2 %copy-start = (f32[5,256]{1,0:T(8,128)S(1)}, f32[5,256]{1,0:T(8,128)}, u32[]{:S(2)}) copy-start(f32[5,256]{1,0:T(8,128)} %param.5) | copy-start | bytes 15364
  1.3 1.7 %copy-start.1 = (bf16[16,64,5,256]{3,1,2,0:T(8,128)(2,1)S(1)}, bf16[16,64,5,256]{3,1,2,0:T(8,128)(2,1)}, u32[]{:S(2)}) copy-start(bf16[16,64,5,256]{3,1,2,0:T(8,128)(2,1)} %param.4) | copy-start | bytes 7864324
  37.8 0.8 %copy-start.2 = (s32[64]{0:T(128)S(1)}, s32[64]{0:T(128)}, u32[]{:S(2)}) copy-start(s32[64]{0:T(128)} %param.7) | copy-start | bytes 772

commit v3 on v2

--- a/solution.py
+++ b/solution.py
@@ -56,40 +56,43 @@
         pl.semaphore_signal(
             barrier, inc=1, device_id={"tm": lax.rem(me + k, count)}, device_id_type=MESH
         )
-    for tile in range(blocks * fields // group):
-        rows = [x_ref[j // fields, j % fields] for j in range(tile * group, (tile + 1) * group)]
-        for d in range(count):
-            packed = jnp.concatenate([r[:, d * sub : (d + 1) * sub] for r in rows], axis=1)
-            send[d, :, tile * LANES : (tile + 1) * LANES] = packed
-    pl.semaphore_wait(barrier, count - 1)
+    chunks, width = send.shape[0], send.shape[3]
+    per_chunk = width // LANES
     copies = []
-    for k in range(1, count):
-        peer = lax.rem(me + k, count)
-        copy = pltpu.make_async_remote_copy(
-            src_ref=send.at[peer],
-            dst_ref=held.at[me],
-            send_sem=send_sem.at[k],
-            recv_sem=recv_sem.at[k],
-            device_id={"tm": peer},
-            device_id_type=MESH,
-        )
-        copy.start()
-        copies.append(copy)
-    held[me] = send[me]
-    for k in range(1, count):
-        source = lax.rem(me + count - k, count)
-        pltpu.make_async_remote_copy(
-            src_ref=send.at[source],
-            dst_ref=held.at[source],
-            send_sem=send_sem.at[k],
-            recv_sem=recv_sem.at[k],
-            device_id={"tm": source},
-            device_id_type=MESH,
-        ).wait_recv()
-    columns = held.shape[2]
-    width = LANES * (5 if (columns // LANES) % 5 == 0 else 1)
-    for c in range(columns // width):
-        part = held[:, :, c * width : (c + 1) * width].reshape(count * steps, width)
+    for c in range(chunks):
+        for tile in range(per_chunk):
+            first = (c * per_chunk + tile) * group
+            rows = [x_ref[j // fields, j % fields] for j in range(first, first + group)]
+            for d in range(count):
+                packed = jnp.concatenate([r[:, d * sub : (d + 1) * sub] for r in rows], axis=1)
+                send[c, d, :, tile * LANES : (tile + 1) * LANES] = packed
+        if c == 0:
+            pl.semaphore_wait(barrier, count - 1)
+        for k in range(1, count):
+            peer = lax.rem(me + k, count)
+            copy = pltpu.make_async_remote_copy(
+                src_ref=send.at[c, peer],
+                dst_ref=held.at[c, me],
+                send_sem=send_sem.at[c, k],
+                recv_sem=recv_sem.at[c, k],
+                device_id={"tm": peer},
+                device_id_type=MESH,
+            )
+            copy.start()
+            copies.append(copy)
+        held[c, me] = send[c, me]
+    for c in range(chunks):
+        for k in range(1, count):
+            source = lax.rem(me + count - k, count)
+            pltpu.make_async_remote_copy(
+                src_ref=send.at[c, source],
+                dst_ref=held.at[c, source],
+                send_sem=send_sem.at[c, k],
+                recv_sem=recv_sem.at[c, k],
+                device_id={"tm": source},
+                device_id_type=MESH,
+            ).wait_recv()
+        part = held[c].reshape(count * steps, width)
         out = jnp.dot(table_ref[...], part, preferred_element_type=jnp.float32)
         spec_ref[:, c * width : (c + 1) * width] = out.astype(jnp.bfloat16)
     for copy in copies:
@@ -99,16 +102,19 @@
 def exchange(by_field, table, count):
     blocks, fields, steps, points = by_field.shape
     columns = blocks * fields * points // count
+    tiles = columns // LANES
+    chunks = tiles // fields if tiles % fields == 0 else 1
+    buffer = pltpu.VMEM((chunks, count, steps, columns // chunks), jnp.bfloat16)
     return pl.pallas_call(
         functools.partial(exchange_kernel, count),
         out_shape=jax.ShapeDtypeStruct((table.shape[0], columns), jnp.bfloat16),
         in_specs=[pl.BlockSpec(memory_space=pltpu.VMEM)] * 2,
         out_specs=pl.BlockSpec(memory_space=pltpu.VMEM),
         scratch_shapes=[
-            pltpu.VMEM((count, steps, columns), jnp.bfloat16),
-            pltpu.VMEM((count, steps, columns), jnp.bfloat16),
-            pltpu.SemaphoreType.DMA((count,)),
-            pltpu.SemaphoreType.DMA((count,)),
+            buffer,
+            buffer,
+            pltpu.SemaphoreType.DMA((chunks, count)),
+            pltpu.SemaphoreType.DMA((chunks, count)),
         ],
         compiler_params=pltpu.CompilerParams(
             collective_id=0, has_side_effects=True, vmem_limit_bytes=VMEM_BYTES

time: 54.2 us -> 54.2 us (level)
    pallas_call x1, Pallas kernels: 14 us -> 13.4 us  [reduce_slots(): pl.pallas_call(functools.partial(reduce_kernel, count, depth), out_shape=...]
    pallas_call x1, Pallas kernels: 32.7 us -> 33.3 us  [exchange(): pl.pallas_call(functools.partial(exchange_kernel, count), out_shape=jax.S...]
where the time goes in v3:
time: 54.2 us; the launch traced here: 54 us
  Pallas kernels  46.7 us (86%)
  local copies, waits for them, and re-layouts  4.44 us (8%)
  other arithmetic  2 us (4%)
  matrix products  0.74 us (1%)
    pallas_call x1, Pallas kernels, exchange(): pl.pallas_call(functools.partial(exchange_kernel, count), out_shape=jax.S...  33.3 us
    pallas_call x1, Pallas kernels, reduce_slots(): pl.pallas_call(functools.partial(reduce_kernel, count, depth), out_shape=...  13.4 us
    unnamed x7, local copies, waits for them, and re-layouts  2.36 us
    reshape x1, local copies, waits for them, and re-layouts, shards(): spectra = spectra.reshape(2, listed, blocks, fields * sub_points)  1.3 us
    convert_element_type x1, other arithmetic, dft_rows(): cosine = (scaled * jnp.cos(angles)).astype(jnp.bfloat16)  1.26 us

profile of v3, /device:TPU:0, one launch (start us, length us, event | category | flops | bytes accessed | tf_op | source)
XLA Modules:
  0.0 54.0 jit_solution(14392369264868045965)
XLA Ops:
  0.0 0.0 copy-start
  0.0 1.3 %multiply_convert_fusion.3 = (bf16[64,512]{1,0:T(8,128)(2,1)S(1)}, bf16[64,512]{1,0:T(8,128)(2,1)S(1)}) fusion(s32[64]{0:T(128)} %param.6, f32[512]{0:T(512)S(1)} %get-tuple-element.9, f32[512]{0:T(512)S(1)} %get-tuple-element.10), kind=kLoop, calls=%fused_computation.17 | loop fusion | flops 589824 | bytes 135424 | tf_op jit(solution)/shard_map/convert_element_type | solution.py:31
  1.3 0.0 copy-start.1
  1.3 1.7 %copy-done.1 = bf16[16,64,5,256]{3,1,2,0:T(8,128)(2,1)S(1)} copy-done((bf16[16,64,5,256]{3,1,2,0:T(8,128)(2,1)S(1)}, bf16[16,64,5,256]{3,1,2,0:T(8,128)(2,1)}, u32[]{:S(2)}) %copy-start.1) | copy-done | bytes 2621464
  3.1 33.3 %shard_map.46 = bf16[128,2560]{1,0:T(8,128)(2,1)S(1)} custom-call(bf16[16,5,64,256]{3,2,1,0:T(8,128)(2,1)S(1)} %bitcast.7, bf16[128,512]{1,0:T(8,128)(2,1)S(1)} %pad_maximum_fusion.table_ref), custom_call_target="tpu_custom_call" | custom-call | tf_op jit(solution)/shard_map/pallas_call | solution.py:108
  36.4 1.3 %reshape.32 = bf16[2,64,16,160]{3,2,1,0:T(8,128)(2,1)S(1)} reshape(bf16[128,2560]{1,0:T(8,128)(2,1)S(1)} %shard_map.46) | data formatting | bytes 1310720 | tf_op jit(solution)/shard_map/reshape | solution.py:205
  37.7 0.1 copy.6
  37.9 0.0 copy-done
  37.9 0.1 constant_dynamic-slice_fusion
  38.0 0.1 mul.81
  38.0 0.4 fusion
  38.5 0.0 copy-start.2
  38.5 0.3 slice_add_fusion
  38.8 0.2 copy.7
  39.1 0.2 copy.8
  39.3 0.0 copy-done.2
  39.3 0.1 fusion.13
  39.4 0.1 reduce_window_sum.11
  39.5 0.2 select_reduce_fusion
  39.7 0.3 fusion.2
  40.0 13.4 %shard_map.47 = f32[16,512]{1,0:T(8,128)S(1)} custom-call(f32[8,16,512]{2,1,0:T(8,128)S(1)} %bitcast.8), custom_call_target="tpu_custom_call" | custom-call | tf_op jit(solution)/shard_map/pallas_call | solution.py:177
  53.4 0.6 %copy.10 = f32[16,512]{1,0:T(8,128)} copy(f32[16,512]{1,0:T(8,128)S(1)} %shard_map.47) | data formatting | bytes 65536
  (3 shorter events, 0.1 us)
Async XLA Ops:
  0.0 37.9 %copy-start = (f32[5,256]{1,0:T(8,128)S(1)}, f32[5,256]{1,0:T(8,128)}, u32[]{:S(2)}) copy-start(f32[5,256]{1,0:T(8,128)} %param.5) | copy-start | bytes 15364
  1.3 1.7 %copy-start.1 = (bf16[16,64,5,256]{3,1,2,0:T(8,128)(2,1)S(1)}, bf16[16,64,5,256]{3,1,2,0:T(8,128)(2,1)}, u32[]{:S(2)}) copy-start(bf16[16,64,5,256]{3,1,2,0:T(8,128)(2,1)} %param.4) | copy-start | bytes 7864324
  38.5 0.8 %copy-start.2 = (s32[64]{0:T(128)S(1)}, s32[64]{0:T(128)}, u32[]{:S(2)}) copy-start(s32[64]{0:T(128)} %param.7) | copy-start | bytes 772

commit v4 on v3

--- a/solution.py
+++ b/solution.py
@@ -11,6 +11,7 @@
 MESH = pl.DeviceIdType.MESH
 LANES = 128
 VMEM_BYTES = 40 * 1024 * 1024
+EXCHANGE_VMEM_BYTES = 60 * 1024 * 1024
 
 
 def slot_index(bin_owners, owner_count):
@@ -46,11 +47,23 @@
     )
 
 
-def exchange_kernel(count, x_ref, table_ref, spec_ref, send, held, send_sem, recv_sem):
+def exchange_kernel(
+    count, x_hbm, table_ref, spec_ref, x_ref, send, held, load_sem, send_sem, recv_sem
+):
     blocks, fields, steps, points = x_ref.shape
     sub = points // count
     group = LANES // sub
     me = lax.axis_index("tm")
+    loads = []
+    rows_each = blocks // send.shape[0]
+    for c in range(send.shape[0]):
+        load = pltpu.make_async_copy(
+            x_hbm.at[pl.ds(c * rows_each, rows_each)],
+            x_ref.at[pl.ds(c * rows_each, rows_each)],
+            load_sem.at[c],
+        )
+        load.start()
+        loads.append(load)
     barrier = pltpu.get_barrier_semaphore()
     for k in range(1, count):
         pl.semaphore_signal(
@@ -60,6 +73,7 @@
     per_chunk = width // LANES
     copies = []
     for c in range(chunks):
+        loads[c].wait()
         for tile in range(per_chunk):
             first = (c * per_chunk + tile) * group
             rows = [x_ref[j // fields, j % fields] for j in range(first, first + group)]
@@ -108,16 +122,21 @@
     return pl.pallas_call(
         functools.partial(exchange_kernel, count),
         out_shape=jax.ShapeDtypeStruct((table.shape[0], columns), jnp.bfloat16),
-        in_specs=[pl.BlockSpec(memory_space=pltpu.VMEM)] * 2,
+        in_specs=[
+            pl.BlockSpec(memory_space=pl.ANY),
+            pl.BlockSpec(memory_space=pltpu.VMEM),
+        ],
         out_specs=pl.BlockSpec(memory_space=pltpu.VMEM),
         scratch_shapes=[
+            pltpu.VMEM(by_field.shape, jnp.bfloat16),
             buffer,
             buffer,
+            pltpu.SemaphoreType.DMA((chunks,)),
             pltpu.SemaphoreType.DMA((chunks, count)),
             pltpu.SemaphoreType.DMA((chunks, count)),
         ],
         compiler_params=pltpu.CompilerParams(
-            collective_id=0, has_side_effects=True, vmem_limit_bytes=VMEM_BYTES
+            collective_id=0, has_side_effects=True, vmem_limit_bytes=EXCHANGE_VMEM_BYTES
         ),
     )(by_field, table)
 

time: 54.2 us -> 56 us (1.033)
  Pallas kernels: 46.7 us -> 48.5 us
  other arithmetic: 2 us -> 2.64 us
  local copies, waits for them, and re-layouts: 4.44 us -> 3.84 us
    pallas_call x1, Pallas kernels: 33.3 us -> 35.3 us  [exchange(): pl.pallas_call(functools.partial(exchange_kernel, count), out_shape=jax.S...]
    unnamed x7 -> x5, local copies, waits for them, and re-layouts: 2.36 us -> 0.63 us
    reshape x1, local copies, waits for them, and re-layouts: 1.3 us -> 2.43 us  [shards(): spectra = spectra.reshape(2, listed, blocks, fields * sub_points)]
    concatenate x1, other arithmetic: 0.01 us -> 0.65 us  [dft_rows(): return jnp.concatenate([cosine, sine_rows], axis=0)]
where the time goes in v4:
time: 56 us; the launch traced here: 55.8 us
  Pallas kernels  48.5 us (87%)
  local copies, waits for them, and re-layouts  3.84 us (7%)
  other arithmetic  2.64 us (5%)
  matrix products  0.74 us (1%)
    pallas_call x1, Pallas kernels, exchange(): pl.pallas_call(functools.partial(exchange_kernel, count), out_shape=jax.S...  35.3 us
    pallas_call x1, Pallas kernels, reduce_slots(): pl.pallas_call(functools.partial(reduce_kernel, count, depth), out_shape=...  13.2 us
    reshape x1, local copies, waits for them, and re-layouts, shards(): spectra = spectra.reshape(2, listed, blocks, fields * sub_points)  2.43 us
    convert_element_type x1, other arithmetic, dft_rows(): cosine = (scaled * jnp.cos(angles)).astype(jnp.bfloat16)  1.26 us

profile of v4, /device:TPU:0, one launch (start us, length us, event | category | flops | bytes accessed | tf_op | source)
XLA Modules:
  0.0 55.8 jit_solution(12791864664392698613)
XLA Ops:
  0.0 0.0 copy-start
  0.0 1.3 %multiply_convert_fusion.3 = (bf16[64,512]{1,0:T(8,128)(2,1)S(1)}, bf16[64,512]{1,0:T(8,128)(2,1)S(1)}) fusion(s32[64]{0:T(128)} %param.6, f32[512]{0:T(512)S(1)} %get-tuple-element.9, f32[512]{0:T(512)S(1)} %get-tuple-element.10), kind=kLoop, calls=%fused_computation.17 | loop fusion | flops 589824 | bytes 135424 | tf_op jit(solution)/shard_map/convert_element_type | solution.py:32
  1.3 0.6 %pad_maximum_fusion.table_ref = bf16[128,512]{1,0:T(8,128)(2,1)} fusion(bf16[64,512]{1,0:T(8,128)(2,1)S(1)} %get-tuple-element.8, bf16[64,512]{1,0:T(8,128)(2,1)S(1)} %get-tuple-element.7), kind=kLoop, calls=%fused_computation.15 | loop fusion | flops 262144 | bytes 262144 | tf_op jit(solution)/shard_map/concatenate | solution.py:34
  2.0 35.3 %shard_map.46 = bf16[128,2560]{1,0:T(8,128)(2,1)} custom-call(bf16[16,5,64,256]{3,2,1,0:T(8,128)(2,1)} %bitcast.10, bf16[128,512]{1,0:T(8,128)(2,1)} %pad_maximum_fusion.table_ref), custom_call_target="tpu_custom_call" | custom-call | tf_op jit(solution)/shard_map/pallas_call | solution.py:122
  37.2 2.4 %reshape.32 = bf16[2,64,16,160]{3,2,1,0:T(8,128)(2,1)S(1)} reshape(bf16[128,2560]{1,0:T(8,128)(2,1)} %shard_map.46) | data formatting | bytes 1310720 | tf_op jit(solution)/shard_map/reshape | solution.py:224
  39.7 0.1 copy.6
  39.8 0.0 copy-done
  39.8 0.1 constant_dynamic-slice_fusion
  39.9 0.1 mul.81
  40.0 0.4 fusion
  40.4 0.0 copy-start.1
  40.4 0.3 slice_add_fusion
  40.8 0.2 copy.7
  41.0 0.2 copy.8
  41.3 0.0 copy-done.1
  41.3 0.1 fusion.13
  41.3 0.1 reduce_window_sum.11
  41.4 0.2 select_reduce_fusion
  41.6 0.3 fusion.2
  42.0 13.2 %shard_map.47 = f32[16,512]{1,0:T(8,128)S(1)} custom-call(f32[8,16,512]{2,1,0:T(8,128)S(1)} %bitcast.7), custom_call_target="tpu_custom_call" | custom-call | tf_op jit(solution)/shard_map/pallas_call | solution.py:196
  55.2 0.6 %copy.10 = f32[16,512]{1,0:T(8,128)} copy(f32[16,512]{1,0:T(8,128)S(1)} %shard_map.47) | data formatting | bytes 65536
  (2 shorter events, 0.1 us)
Async XLA Ops:
  0.0 39.8 %copy-start = (f32[5,256]{1,0:T(8,128)S(1)}, f32[5,256]{1,0:T(8,128)}, u32[]{:S(2)}) copy-start(f32[5,256]{1,0:T(8,128)} %param.5) | copy-start | bytes 15364
  40.4 0.8 %copy-start.1 = (s32[64]{0:T(128)S(1)}, s32[64]{0:T(128)}, u32[]{:S(2)}) copy-start(s32[64]{0:T(128)} %param.7) | copy-start | bytes 772
